TPU v7x, 256 devices: a whole 4x4x8 slice. The times are simulated.
256 devices in a mesh: replica: 8 (over x, y_lo), tensor: 32 (over z, y_hi, core).
Axes of the slice: x: 4, y: 4 (y_hi: 2, y_lo: 2; y = y_hi * 2 + y_lo), z: 8, core: 2. Of those that a mesh axis runs over, the one named last changes fastest.
Arguments:
- inputs: bfloat16 [8, 1280, 2304], P('replica', 'tensor'), may hold values from -6 to 6
- cotangent: bfloat16 [8, 1280, 2304], P('replica', 'tensor'), may hold values from -6 to 6
- gate_weight: bfloat16 [8, 2304, 9216], P('replica', None, 'tensor'), may hold values from -6 to 6
- up_weight: bfloat16 [8, 2304, 9216], P('replica', None, 'tensor'), may hold values from -6 to 6
- down_weight: bfloat16 [8, 9216, 2304], P('replica', 'tensor'), may hold values from -6 to 6
- step: int32 [1], replicated, may hold values from 0 to 2999
Outputs:
- input_grad: bfloat16 [8, 1280, 2304], P('replica', 'tensor')
- gate_next: bfloat16 [8, 2304, 9216], P('replica', None, 'tensor')
- up_next: bfloat16 [8, 2304, 9216], P('replica', None, 'tensor')
- down_next: bfloat16 [8, 9216, 2304], P('replica', 'tensor')
All inputs are finite; a program needn't handle non-finite values.
Results may differ from a plain program's by a relative error of at most 0.0052.
Values may be sent and summed in bfloat16 or wider, within the bound.
A program may use at most 128 MiB of HBM per device.

v0:
```python
import math

import jax
import jax.numpy as jnp
from jax import lax
from jax.sharding import PartitionSpec as P

D = 2304
FF = 9216


gelu_c = 0.7978845608028654
gelu_k = 0.044715
learn_rate = 1.0


def shifted(array, axis, by):
    peers = lax.axis_size(axis)
    return lax.ppermute(array, axis, [(i, (i + by) % peers) for i in range(peers)])


def gelu_parts(value):
    inner = gelu_c * (value + gelu_k * value * value * value)
    tangent = jnp.tanh(inner)
    act = 0.5 * value * (1.0 + tangent)
    slope = 0.5 * (1.0 + tangent) + 0.5 * value * (1.0 - tangent * tangent) * gelu_c * (
        1.0 + 3.0 * gelu_k * value * value
    )
    return (act, slope)


def contract_rows(left, right):
    return lax.dot_general(
        left, right, (((0,), (0,)), ((), ())), preferred_element_type=jnp.float32
    )


def contract_cols(left, right):
    return lax.dot_general(
        left, right, (((1,), (1,)), ((), ())), preferred_element_type=jnp.float32
    )


def stepped(weight, grad):
    return (weight.astype(jnp.float32) - learn_rate * grad).astype(jnp.bfloat16)


def gossip(arrays, step):
    size = lax.axis_size("replica")
    level = step[0] % 3

    def make(distance):
        offset = distance % size

        def moved():
            return [shifted(item, "replica", -offset) for item in arrays]

        return moved

    peers = lax.switch(level, [make(1 << power) for power in range(3)])
    return [
        ((own.astype(jnp.float32) + other.astype(jnp.float32)) * 0.5).astype(jnp.bfloat16)
        for own, other in zip(arrays, peers)
    ]


def body(inputs, cotangent, gate_weight, up_weight, down_weight, step):
    rows = inputs[0]
    out_rows = cotangent[0]
    w_gate = gate_weight[0]
    w_up = up_weight[0]
    w_down = down_weight[0]
    scale_model = 1.0 / math.sqrt(D)
    scale_hidden = 1.0 / math.sqrt(FF)
    whole = lax.all_gather(rows, "tensor", axis=0, tiled=True)
    gate = jnp.dot(whole, w_gate, preferred_element_type=jnp.float32) * scale_model
    up = jnp.dot(whole, w_up, preferred_element_type=jnp.float32) * scale_model
    act, slope = gelu_parts(gate)
    hidden = (act * up).astype(jnp.bfloat16)
    whole_grad = lax.all_gather(out_rows, "tensor", axis=0, tiled=True)
    hidden_grad = contract_cols(whole_grad, w_down) * scale_hidden
    gate_grad = (hidden_grad * up * slope).astype(jnp.bfloat16)
    up_grad = (hidden_grad * act).astype(jnp.bfloat16)
    term = (contract_cols(gate_grad, w_gate) + contract_cols(up_grad, w_up)) * scale_model
    columns = lax.psum_scatter(term, "tensor", scatter_dimension=1, tiled=True).astype(jnp.bfloat16)
    grad_rows = lax.all_to_all(columns, "tensor", split_axis=0, concat_axis=1, tiled=True)
    sum_gate = contract_rows(whole, gate_grad)
    sum_up = contract_rows(whole, up_grad)
    new_gate = stepped(w_gate, sum_gate * scale_model)
    new_up = stepped(w_up, sum_up * scale_model)
    new_down = stepped(w_down, contract_rows(hidden, whole_grad) * scale_hidden)
    paired, down_avg = gossip([jnp.stack([new_gate, new_up]), new_down], step)
    gate_avg, up_avg, down_avg = (paired[0], paired[1], down_avg)
    return (grad_rows[None], gate_avg[None], up_avg[None], down_avg[None])


def solution(mesh):
    in_specs = (
        P("replica", "tensor", None),
        P("replica", "tensor", None),
        P("replica", None, "tensor"),
        P("replica", None, "tensor"),
        P("replica", "tensor", None),
        P(),
    )
    out_specs = (
        P("replica", "tensor", None),
        P("replica", None, "tensor"),
        P("replica", None, "tensor"),
        P("replica", "tensor", None),
    )
    return jax.shard_map(body, mesh=mesh, in_specs=in_specs, out_specs=out_specs, check_vma=False)
```

profile of v0, /device:TPU:1, one launch (start us, length us, event | category | flops | bytes accessed | tf_op | source)
XLA Modules:
  0.0 460.8 jit_solution(11440124262467791313)
XLA Ops:
  7.2 0.0 all-gather.7.cloned.1.call-start
  7.2 0.7 all-gather.7.cloned.1.call-update
  7.9 0.0 all-gather.5.cloned.1.call-start
  7.9 0.7 all-gather.5.cloned.1.call-update
  8.7 0.0 reduce-scatter.2.cloned.1.call-start
  8.7 99.2 %all-gather.7.cloned.1.call-done = bf16[1,1280,2304]{2,1,0:T(8,128)(2,1)} async-done(((bf16[1,40,2304]{2,1,0:T(8,128)(2,1)}), bf16[1,1280,2304]{2,1,0:T(8,128)(2,1)}) %all-gather.7.cloned.1.call-update) | async-done | bytes 5898256 | tf_op jit(solution)/shard_map/all_gather | solution.py:75
  107.9 6.3 %fusion.5 = f32[1280,288]{0,1:T(8,128)} fusion(bf16[1,1280,2304]{2,1,0:T(8,128)(2,1)} %all-gather.7.cloned.1.call-done, bf16[1,2304,288]{1,2,0:T(8,128)(2,1)} %param.11), kind=kOutput, calls=%fused_computation.6 | convolution fusion | flops 1698693120 | bytes 8699904 | tf_op jit(solution)/shard_map/dot_general | solution.py:76
  114.2 3.1 fusion.57
  117.4 83.0 %all-gather.5.cloned.1.call-done = bf16[1,1280,2304]{2,1,0:T(8,128)(2,1)} async-done(((bf16[1,40,2304]{2,1,0:T(8,128)(2,1)}), bf16[1,1280,2304]{2,1,0:T(8,128)(2,1)}) %all-gather.5.cloned.1.call-update) | async-done | bytes 5898256 | tf_op jit(solution)/shard_map/all_gather | solution.py:80
  200.4 6.4 %multiply_convert_fusion.1 = (bf16[1280,288]{0,1:T(8,128)(2,1)S(1)}, bf16[1280,288]{0,1:T(8,128)(2,1)S(1)}) fusion(f32[1280,288]{0,1:T(8,128)} %fusion.5, f32[1280,288]{0,1:T(8,128)} %fusion.57, bf16[1,288,2304]{2,1,0:T(8,128)(2,1)} %param.13, bf16[1,1280,2304]{2,1,0:T(8,128)(2,1)} %all-gather.5.cloned.1.call-done), kind=kOutput, calls=%fused_computation.40 | convolution fusion | flops 1707909120 | bytes 11649024 | tf_op jit(solution)/shard_map/dot_general | solution.py:39
  206.8 3.3 fusion.67
  210.2 6.6 %fusion = f32[1280,2304]{0,1:T(8,128)} fusion(f32[1280,2304]{0,1:T(8,128)S(1)} %fusion.67, bf16[1280,288]{0,1:T(8,128)(2,1)S(1)} %get-tuple-element.62, bf16[1,2304,288]{1,2,0:T(8,128)(2,1)S(1)} %copy-done), kind=kOutput, calls=%fused_computation.1 | convolution fusion | flops 1704591360 | bytes 25657344 | tf_op jit(solution)/shard_map/dot_general | solution.py:39
  217.5 4.7 %fusion.51 = bf16[1,2304,288]{1,2,0:T(8,128)(2,1)S(1)} fusion(bf16[1280,288]{0,1:T(8,128)(2,1)S(1)} %get-tuple-element.62, bf16[1,1280,2304]{2,1,0:T(8,128)(2,1)} %all-gather.7.cloned.1.call-done, bf16[1,2304,288]{1,2,0:T(8,128)(2,1)S(1)} %copy-done), kind=kOutput, calls=%fused_computation.29 | convolution fusion | flops 1701347328 | bytes 9289728 | tf_op jit(solution)/shard_map/dot_general | solution.py:33
  222.2 5.0 %fusion.48 = bf16[1,2304,288]{1,2,0:T(8,128)(2,1)S(1)} fusion(bf16[1280,288]{0,1:T(8,128)(2,1)S(1)} %copy-done.4, bf16[1,1280,2304]{2,1,0:T(8,128)(2,1)} %all-gather.7.cloned.1.call-done, bf16[1,2304,288]{1,2,0:T(8,128)(2,1)S(1)} %copy-done.2), kind=kOutput, calls=%fused_computation.28 | convolution fusion | flops 1701347328 | bytes 9289728 | tf_op jit(solution)/shard_map/dot_general | solution.py:33
  227.3 0.2 pad_maximum_fusion
  227.5 1.1 copy-done.6
  228.6 0.6 copy-done.7
  229.2 0.5 copy-done.8
  229.7 3.3 fusion.39
  233.1 109.6 %conditional.4 = (bf16[2,2304,288]{1,2,0:T(8,128)(2,1)}, bf16[288,2304]{1,0:T(8,128)(2,1)}) conditional(s32[]{:T(128)} %clamp.3, (bf16[2,2304,288]{1,2,0:T(8,128)(2,1)S(1)}, bf16[288,2304]{1,0:T(8,128)(2,1)}) %tuple.40, (bf16[2,2304,288]{1,2,0:T(8,128)(2,1)S(1)}, bf16[288,2304]{1,0:T(8,128)(2,1)}) %tuple.40, ...), branch_computations={%region_1.2_spmd, %region_2.3_spmd, %region_3.4_spmd} | conditional | bytes 15925344
  233.1 2.2 collective-permute-start
  235.2 1.4 collective-permute-start.1
  236.7 106.0 %collective-permute-done.1 = bf16[288,2304]{1,0:T(8,128)(2,1)} collective-permute-done((bf16[288,2304]{1,0:T(8,128)(2,1)}, bf16[288,2304]{1,0:T(8,128)(2,1)}, u32[]{:S(2)}, u32[]{:S(2)}) %collective-permute-start.1) | collective-permute-done | bytes 1327136 | tf_op jit(solution)/shard_map/cond/branch_0_fun/ppermute | solution.py:19
  342.6 2.6 fusion.14
  345.2 1.7 fusion.79
  346.9 80.7 %reduce-scatter.2.cloned.1.call-done = f32[1280,72]{0,1:T(8,128)} async-done(((f32[1280,2304]{0,1:T(8,128)}), f32[1280,72]{0,1:T(8,128)}) %reduce-scatter.2.cloned.1.call-update) | async-done | bytes 368656 | tf_op jit(solution)/shard_map/reduce_scatter | solution.py:85
  427.6 1.0 convert_element_type.66
  428.6 0.9 copy.26
  429.5 10.3 %all-to-all-start = ((bf16[32,40,72]{2,1,0:T(8,128)(2,1)}), bf16[32,40,72]{2,1,0:T(8,128)(2,1)S(1)}, u32[]{:S(2)}, u32[]{:S(2)}) async-start(bf16[32,40,72]{2,1,0:T(8,128)(2,1)} %bitcast.5), calls=%async_computation.1 | async-start | bytes 655360 | tf_op jit(solution)/shard_map/all_to_all | solution.py:86
  439.8 3.2 fusion.66
  443.0 10.1 %all-to-all-done = bf16[32,40,72]{2,1,0:T(8,128)(2,1)S(1)} async-done(((bf16[32,40,72]{2,1,0:T(8,128)(2,1)}), bf16[32,40,72]{2,1,0:T(8,128)(2,1)S(1)}, u32[]{:S(2)}, u32[]{:S(2)}) %all-to-all-start) | async-done | bytes 184352 | tf_op jit(solution)/shard_map/all_to_all | solution.py:86
  453.2 1.1 broadcast_in_dim.6
  (23 shorter events, 0.1 us)
Async XLA Ops:
  7.2 100.8 %all-gather.7.cloned.1.call-start = ((), (), s32[]{:S(2)}) async-start(), calls=%async_computation.4 | async-start | bytes 6082560 | tf_op jit(solution)/shard_map/all_gather | solution.py:75
  7.9 192.5 %all-gather.5.cloned.1.call-start = ((), (), s32[]{:S(2)}) async-start(), calls=%async_computation.3 | async-start | bytes 6082560 | tf_op jit(solution)/shard_map/all_gather | solution.py:80
  8.7 105.6 %copy-start = (bf16[1,2304,288]{1,2,0:T(8,128)(2,1)S(1)}, bf16[1,2304,288]{1,2,0:T(8,128)(2,1)}, u32[]{:S(2)}) copy-start(bf16[1,2304,288]{1,2,0:T(8,128)(2,1)} %param.12) | copy-start | bytes 3981316
  8.7 418.9 %reduce-scatter.2.cloned.1.call-start = ((), (), s32[]{:S(2)}) async-start(), calls=%async_computation.2 | async-start | bytes 12165120 | tf_op jit(solution)/shard_map/reduce_scatter | solution.py:85
  107.9 6.3 %copy-start.5 = (bf16[1,1280,2304]{2,1,0:T(8,128)(2,1)S(1)}, bf16[1,1280,2304]{2,1,0:T(8,128)(2,1)}, u32[]{:S(2)}) copy-start(bf16[1,1280,2304]{2,1,0:T(8,128)(2,1)} %all-gather.7.cloned.1.call-done) | copy-start | bytes 17694724
  117.4 89.5 %copy-start.1 = (bf16[1,2304,288]{1,2,0:T(8,128)(2,1)S(1)}, bf16[1,2304,288]{1,2,0:T(8,128)(2,1)}, u32[]{:S(2)}) copy-start(bf16[1,2304,288]{1,2,0:T(8,128)(2,1)} %param.11) | copy-start | bytes 3981316
  206.8 3.3 copy-start.3
  217.5 4.8 %copy-start.2 = (bf16[1,2304,288]{1,2,0:T(8,128)(2,1)S(1)}, bf16[1,2304,288]{1,2,0:T(8,128)(2,1)}, u32[]{:S(2)}) copy-start(bf16[1,2304,288]{1,2,0:T(8,128)(2,1)} %param.11) | copy-start | bytes 3981316
  217.5 4.8 %copy-start.4 = (bf16[1280,288]{0,1:T(8,128)(2,1)S(1)}, bf16[1280,288]{0,1:T(8,128)(2,1)}, u32[]{:S(2)}) copy-start(bf16[1280,288]{0,1:T(8,128)(2,1)} %copy-done.3) | copy-start | bytes 2211844
  217.5 10.0 %slice-start = ((s8[5898240]{0:T(1024)(128)(4,1)}), s8[4194304]{0:T(1024)(128)(4,1)S(1)}, s32[]{:S(2)}) async-start(s8[5898240]{0:T(1024)(128)(4,1)} %bitcast.94), calls=%async_computation.5 | async-start | bytes 8388608
  222.2 5.3 %slice-start.1 = ((s8[5898240]{0:T(1024)(128)(4,1)}), s8[1703936]{0:T(1024)(128)(4,1)S(1)}, s32[]{:S(2)}) async-start(s8[5898240]{0:T(1024)(128)(4,1)} %bitcast.94), calls=%async_computation.6 | async-start | bytes 3407872
  227.2 1.4 copy-start.6
  227.2 2.0 copy-start.7
  227.2 2.5 copy-start.8
  233.1 109.6 %collective-permute-start = (bf16[2,2304,288]{1,2,0:T(8,128)(2,1)S(1)}, bf16[2,2304,288]{1,2,0:T(8,128)(2,1)}, u32[]{:S(2)}, u32[]{:S(2)}) collective-permute-start(bf16[2,2304,288]{1,2,0:T(8,128)(2,1)S(1)} %get-tuple-element.24), channel_id=1, source_target_pairs={{0,224},{32,0},{64,32},{96,64},{128,96},{160,128},{192,160},{224,1... | collective-permute-start | bytes 7962632 | tf_op jit(solution)/shard_map/cond/branch_0_fun/ppermute | solution.py:19
  235.2 107.4 %collective-permute-start.1 = (bf16[288,2304]{1,0:T(8,128)(2,1)}, bf16[288,2304]{1,0:T(8,128)(2,1)}, u32[]{:S(2)}, u32[]{:S(2)}) collective-permute-start(bf16[288,2304]{1,0:T(8,128)(2,1)} %get-tuple-element.25), channel_id=1, source_target_pairs={{0,224},{32,0},{64,32},{96,64},{128,96},{160,128},{192,160},{224,1... | collective-permute-start | bytes 3981320 | tf_op jit(solution)/shard_map/cond/branch_0_fun/ppermute | solution.py:19
  429.5 23.6 %all-to-all-start = ((bf16[32,40,72]{2,1,0:T(8,128)(2,1)}), bf16[32,40,72]{2,1,0:T(8,128)(2,1)S(1)}, u32[]{:S(2)}, u32[]{:S(2)}) async-start(bf16[32,40,72]{2,1,0:T(8,128)(2,1)} %bitcast.5), calls=%async_computation.1 | async-start | bytes 655360 | tf_op jit(solution)/shard_map/all_to_all | solution.py:86
Sparse Core Ops, SparseCore 0:
  10.7 97.1 all-gather.6
  110.7 89.6 all-gather.4
  216.9 210.6 reduce-scatter.1
where the time goes:
time: 461 us
  waiting for transfers between devices  380 us (82%)
  matrix products  38.8 us (8%)
  between operations  14.6 us (3%)
  starting transfers between devices  14 us (3%)
  other arithmetic  6.99 us (2%)
  local copies, waits for them, and re-layouts  5.96 us (1%)
    ppermute x2, waiting for transfers between devices, shifted(): lax.ppermute(array, axis, [(i, (i + by) % peers) for i in range(peers)])  106 us
    all_gather x1, waiting for transfers between devices, body(): whole = lax.all_gather(rows, 'tensor', axis=0, tiled=True)  99.2 us
    all_gather x1, waiting for transfers between devices, body(): whole_grad = lax.all_gather(out_rows, 'tensor', axis=0, tiled=True)  83 us
    reduce_scatter x1, waiting for transfers between devices, body(): lax.psum_scatter(term, 'tensor', scatter_dimension=1, tiled=True)  80.7 us
    dot_general x3, matrix products, contract_cols(): lax.dot_general(left, right, (((1,), (1,)), ((), ())), preferred_element_...  16.4 us
    dot_general x3, matrix products, contract_rows(): lax.dot_general(left, right, (((0,), (0,)), ((), ())), preferred_element_...  13 us
    all_to_all x1, starting transfers between devices, body(): lax.all_to_all(columns, 'tensor', split_axis=0, concat_axis=1, tiled=True)  10.3 us
    all_to_all x1, waiting for transfers between devices, body(): lax.all_to_all(columns, 'tensor', split_axis=0, concat_axis=1, tiled=True)  10.1 us
  transfers between devices with their start and end apart: 6, of which 5 were waited for; matrix products, arithmetic and copies ran while one was open for 7% of the time, Pallas kernels for 0%

commit v1 on v0

v1 whole, which is shorter than its diff:
```python
import functools
import math

import jax
import jax.numpy as jnp
from jax import lax
from jax.experimental import pallas as pl
from jax.experimental.pallas import tpu as pltpu
from jax.sharding import PartitionSpec as P

D = 2304
FF = 9216
TOKENS = 1280
UNITS = 288
WIDE = 384
BLOCK = 80
PAIR = 160
HALF = D // 2
PIECE = 256
PIECES = D // PIECE
EARLY = 4
LONG = 2

gelu_c = 0.7978845608028654
gelu_k = 0.044715
learn_rate = 1.0
scale_model = 1.0 / math.sqrt(D)
scale_hidden = 1.0 / math.sqrt(FF)

MESH = pl.DeviceIdType.MESH
F32 = jnp.float32
BF16 = jnp.bfloat16


def gelu_parts(value):
    inner = gelu_c * (value + gelu_k * value * value * value)
    tangent = jnp.tanh(inner)
    act = 0.5 * value * (1.0 + tangent)
    slope = 0.5 * (1.0 + tangent) + 0.5 * value * (1.0 - tangent * tangent) * gelu_c * (
        1.0 + 3.0 * gelu_k * value * value
    )
    return act, slope


def dot(left, right, dims):
    return lax.dot_general(left, right, (dims, ((), ())), preferred_element_type=F32)


def place_behind(k):
    return jnp.maximum(2 * k - 1, 0)


def place_ahead(k):
    return jnp.minimum(2 * k, 7)


def block_rows(place, pair):
    return pl.ds(pl.multiple_of(place * PAIR + BLOCK * pair, 16), BLOCK)


def pair_rows(place):
    return pl.ds(pl.multiple_of(place * PAIR, 16), PAIR)


def loop(first, end, step):
    def one(i, carry):
        step(i)
        return carry

    lax.fori_loop(first, end, one, 0)


def kernel(
    distance,
    x_in, cot_in, wg_in, wu_in, wd_in,
    grad_out, gate_out, up_out, down_out,
    xs, cs, weights, gu, hid, turned, gate_up, part, part_sib, lead, chain, new_buf, peer_buf, relay,
    wide32, pair32, ysend, ybuf, fin, rows32,
    load_sem, pair_ss, pair_rs, zx_ss, zx_rs, zc_ss, zc_rs, yx_ss, yx_rs, yc_ss, yc_rs,
    sx_ss, sx_rs, sc_ss, sc_rs, p_ss, p_rs, ch_ss, ch_rs, ys_ss, ys_rs, f_ss, f_rs,
    g_ss, g_rs, out_sem, r_ss, r_rs,
):
    r = lax.axis_index("replica")
    t = lax.axis_index("tensor")
    z, yh, c = t // 4, (t // 2) % 2, t % 2
    base = yh * 2 + c
    ahead = (r, lax.rem(z + 1, 8) * 4 + base)
    behind = (r, lax.rem(z + 7, 8) * 4 + base)
    across = (r, z * 4 + (1 - yh) * 2 + c)
    sibling = (r, z * 4 + yh * 2 + (1 - c))
    gives_to = (lax.rem(r + 8 - distance, 8), t)
    takes_from = (lax.rem(r + distance, 8), t)

    long = LONG if distance == 2 else 0
    onward = (r, lax.rem(z + 1 + 6 * c, 8) * 4 + base)
    backward_on = (r, lax.rem(z + 7 - 6 * c, 8) * 4 + base)

    mine = pl.ds(pl.multiple_of(c * HALF, 128), HALF)
    other = pl.ds(pl.multiple_of((1 - c) * HALF, 128), HALF)

    def remote(src, dst, ss, rs, device):
        return pltpu.make_async_remote_copy(
            src_ref=src, dst_ref=dst, send_sem=ss, recv_sem=rs, device_id=device, device_id_type=MESH
        )

    loads = [
        pltpu.make_async_copy(source.at[0], weights.at[pl.ds(WIDE * i, UNITS), :], load_sem.at[i])
        for i, source in enumerate((wg_in, wu_in, wd_in))
    ]
    for load in loads:
        load.start()

    barrier = pltpu.get_barrier_semaphore()
    senders = (ahead, behind, across, sibling, takes_from) + ((gives_to,) if long else ())
    for device in senders:
        pl.semaphore_signal(barrier, inc=1, device_id=device, device_id_type=MESH)
    wide32[0] = x_in[0].astype(F32)
    wide32[1] = cot_in[0].astype(F32)
    pl.semaphore_wait(barrier, len(senders))

    forty = pl.ds(pl.multiple_of(c * 40, 8), 40)
    pairs = [
        remote(wide32.at[a, :, other], pair32.at[a, forty, :], pair_ss.at[a], pair_rs.at[a], sibling) for a in range(2)
    ]
    for copy in pairs:
        copy.start()
    for a in range(2):
        pair32[a, forty, :] = wide32[a, :, mine]

    def first_place(k):
        return jnp.where(c == 0, place_behind(k), place_ahead(k))

    def second_place(k):
        return jnp.where(c == 0, place_ahead(k), place_behind(k))

    def hop(buf, ss, rs, forward, k, pair):
        place = first_place if forward else second_place
        slot = 2 * place(k) + pair
        return remote(
            buf.at[block_rows(place(k - 1), pair), mine], buf.at[block_rows(place(k), pair), mine],
            ss.at[slot], rs.at[slot], onward if forward else backward_on,
        )

    def x_hop(forward, k):
        return hop(xs, zx_ss, zx_rs, forward, k, 0)

    def c_hop(forward, k, pair):
        return hop(cs, zc_ss, zc_rs, forward, k, pair)

    def x_across(place):
        return remote(
            xs.at[block_rows(place, 0), mine], xs.at[block_rows(place, 1), mine],
            yx_ss.at[place], yx_rs.at[place], across,
        )

    c_across = remote(cs.at[block_rows(0, 0), mine], cs.at[block_rows(0, 1), mine], yc_ss, yc_rs, across)

    def x_sibling(place):
        at = xs.at[pair_rows(place), mine]
        return remote(at, at, sx_ss.at[place], sx_rs.at[place], sibling)

    def c_sibling(place):
        at = cs.at[pair_rows(place), mine]
        return remote(at, at, sc_ss.at[place], sc_rs.at[place], sibling)

    def part_sibling(place):
        rows = pair_rows(place)
        return remote(part.at[rows, other], part_sib.at[rows, :], p_ss.at[place], p_rs.at[place], sibling)

    pairs[0].wait_recv()
    xs[pl.ds(0, BLOCK), mine] = pair32[0].astype(BF16)
    x_hop(True, 1).start()
    x_hop(False, 1).start()
    x_across(0).start()
    pairs[1].wait_recv()
    cs[pl.ds(0, BLOCK), mine] = pair32[1].astype(BF16)
    c_across.start()

    for i in range(3):
        weights[pl.ds(WIDE * i + UNITS, WIDE - UNITS), :] = jnp.zeros((WIDE - UNITS, D), BF16)
    for load in loads:
        load.wait()

    def forward_a(place):
        x_sibling(place).wait_recv()
        gate_up[lax.rem(place, 4)] = dot(xs[pair_rows(place), :], weights[pl.ds(0, 2 * WIDE), :], ((1,), (1,)))

    def forward_b(place):
        c_sibling(place).wait_recv()
        at = lax.rem(place, 4)
        rows = pair_rows(place)
        hidden_grad = dot(cs[rows, :], weights[pl.ds(2 * WIDE, WIDE), :], ((1,), (1,))) * scale_hidden
        gate = gate_up[at, :, pl.ds(0, WIDE)] * scale_model
        up = gate_up[at, :, pl.ds(WIDE, WIDE)] * scale_model
        act, slope = gelu_parts(gate)
        hid[rows, :] = (act * up).astype(BF16)
        gu[rows, pl.ds(0, WIDE)] = (hidden_grad * up * slope).astype(BF16)
        gu[rows, pl.ds(WIDE, WIDE)] = (hidden_grad * act).astype(BF16)

    def turn(b):
        rows = pl.ds(pl.multiple_of(b * 128, 128), 128)
        turned[pl.ds(0, UNITS), rows] = gu[rows, pl.ds(0, WIDE)].T[0:UNITS]
        turned[pl.ds(UNITS, UNITS), rows] = gu[rows, pl.ds(WIDE, WIDE)].T[0:UNITS]
        turned[pl.ds(2 * UNITS, UNITS), rows] = hid[rows, :].T[0:UNITS]

    def turn_pair(place):
        loop((PAIR * place) // 128, (PAIR * (place + 1)) // 128, turn)

    def backward(place):
        rows = pair_rows(place)

        def columns(j):
            cols = pl.ds(pl.multiple_of(j * 768, 768), 768)
            part[rows, cols] = dot(gu[rows, :], weights[pl.ds(0, 2 * WIDE), cols], ((1,), (0,)))

        loop(0, 3, columns)
        part_sibling(place).start()

    def gossip(j):
        return remote(new_buf.at[j], peer_buf.at[j], g_ss.at[j], g_rs.at[j], gives_to)

    def goes_long(j):
        return jnp.logical_and(j >= 1, j <= long)

    def long_way(hop_number, j):
        src = new_buf.at[j] if hop_number == 0 else relay.at[hop_number - 1, j - 1]
        if hop_number == 2:
            return remote(src, peer_buf.at[j], r_ss.at[2, j - 1], g_rs.at[j], takes_from)
        return remote(
            src, relay.at[hop_number, j - 1], r_ss.at[hop_number, j - 1], r_rs.at[hop_number, j - 1], takes_from
        )

    def pass_on(hop_number):
        def one(j):
            long_way(hop_number - 1, j).wait_recv()
            long_way(hop_number, j).start()

        loop(1, long + 1, one)

    def update(j):
        cols = pl.ds(pl.multiple_of(j * PIECE, PIECE), PIECE)
        sums = dot(turned[pl.ds(0, 2 * UNITS), :], xs[:, cols], ((1,), (0,))) * scale_model
        for i in range(2):
            old = weights[pl.ds(WIDE * i, UNITS), cols].astype(F32)
            new_buf[j, pl.ds(UNITS * i, UNITS), :] = (old - learn_rate * sums[UNITS * i : UNITS * (i + 1)]).astype(BF16)
        sums = dot(turned[pl.ds(2 * UNITS, UNITS), :], cs[:, cols], ((1,), (0,))) * scale_hidden
        old = weights[pl.ds(2 * WIDE, UNITS), cols].astype(F32)
        new_buf[j, pl.ds(2 * UNITS, UNITS), :] = (old - learn_rate * sums).astype(BF16)
        if long:
            @pl.when(goes_long(j))
            def _():
                long_way(0, j).start()

            pl.when(jnp.logical_not(goes_long(j)))(lambda: gossip(j).start())
        else:
            gossip(j).start()

    chains = ((True, 0, 4), (True, 1, 3), (False, 0, 3), (False, 1, 4))

    def stop_place(n, m):
        onward = chains[n][2] - m
        return place_ahead(onward) if chains[n][0] else place_behind(onward)

    def chain_hop(n, m, src):
        return remote(src, chain.at[n, m], ch_ss.at[n, m], ch_rs.at[n, m], ahead if chains[n][0] else behind)

    def add_share(dst, src, place, pair):
        def some(i):
            at = pl.ds(pl.multiple_of(i * 16, 16), 16)
            rows = pl.ds(pl.multiple_of(place * PAIR + BLOCK * pair + i * 16, 16), 16)
            share = part[rows, mine] + part_sib[rows, :]
            dst[at, :] = (share if src is None else src(at) + share).astype(dst.dtype)

        loop(0, BLOCK // 16, some)

    def start_chains():
        for p in (5, 6, 7):
            part_sibling(p).wait_recv()
        for n, (_, pair, _) in enumerate(chains):
            place = stop_place(n, 0)
            add_share(lead.at[n], None, place, pair)
            chain_hop(n, 0, lead.at[n]).start()

    def places(k, work):
        loop(jnp.maximum(2 * k - 1, 0), jnp.where(k < 0, 0, jnp.minimum(2 * k + 1, 8)), work)

    def step(k):
        @pl.when(k <= 4)
        def _():
            x_hop(True, k).wait_recv()

            @pl.when(k <= 3)
            def _():
                x_hop(True, k + 1).start()

            x_across(first_place(k)).start()

            @pl.when(k <= 3)
            def _():
                x_hop(False, k).wait_recv()

                @pl.when(k <= 2)
                def _():
                    x_hop(False, k + 1).start()

                x_across(second_place(k)).start()

        def from_across(place):
            x_across(place).wait_recv()
            x_sibling(place).start()

        def take_c(forward, pair):
            far = forward == (pair == 0)

            @pl.when(k <= (5 if far else 4))
            def _():
                @pl.when(k >= 2)
                def _():
                    c_hop(forward, k - 1, pair).wait_recv()

                @pl.when(k <= (4 if far else 3))
                def _():
                    c_hop(forward, k, pair).start()

        places(k - 1, from_across)
        take_c(True, 0)
        take_c(False, 0)
        places(k - 1, forward_a)
        places(k - 2, forward_b)

        @pl.when(k == 1)
        def _():
            c_across.wait_recv()

        take_c(False, 1)
        take_c(True, 1)
        places(k - 1, lambda place: c_sibling(place).start())
        places(k - 2, turn_pair)

        @pl.when(k == 7)
        def _():
            backward(7)
            start_chains()

        loop(jnp.where(k == 7, EARLY, 0), jnp.where(k == 7, PIECES, jnp.where(k == 6, EARLY, 0)), update)

        @pl.when(k < 7)
        def _():
            places(k - 3, backward)

    loop(1, 8, step)

    for p in range(5):
        part_sibling(p).wait_recv()

    def chain_step(m):
        for n, (_, pair, stops) in enumerate(chains):
            def go(n=n, pair=pair):
                at = chain.at[n, m - 1]
                chain_hop(n, m - 1, at).wait_recv()
                add_share(at, lambda i: at[i, :].astype(F32), stop_place(n, m), pair)
                chain_hop(n, m, at).start()

            if stops == 4:
                go()
            elif isinstance(m, int):
                if m < stops:
                    go()
            else:
                pl.when(m < stops)(go)

    if long:
        loop(1, 3, chain_step)
        pass_on(1)
        chain_step(3)
    else:
        loop(1, 4, chain_step)
    for n in (1, 3):
        chain_hop(n, chains[n][2] - 1, chain.at[n, 0]).wait_recv()
    add_share(ysend, lambda i: chain[1, 2, i, :].astype(F32) + chain[3, 3, i, :].astype(F32), 0, 1)
    y_sum = remote(ysend, ybuf, ys_ss, ys_rs, across)
    y_sum.start()
    for n in (0, 2):
        chain_hop(n, chains[n][2] - 1, chain.at[n, 0]).wait_recv()
    add_share(fin, lambda i: chain[0, 3, i, :].astype(F32) + chain[2, 2, i, :].astype(F32), 0, 0)
    y_sum.wait_recv()
    fin[...] = (fin[...] + ybuf[...]) * scale_model
    theirs = pl.ds(pl.multiple_of((1 - c) * 40, 8), 40)
    rows_fly = remote(fin.at[theirs, :], rows32.at[:, mine], f_ss, f_rs, sibling)
    rows_fly.start()
    rows32[:, mine] = fin[forty, :]
    rows_fly.wait_recv()
    grad_out[0] = rows32[...].astype(BF16)

    def outs(j):
        cols = pl.ds(pl.multiple_of(j * PIECE, PIECE), PIECE)
        return [
            pltpu.make_async_copy(peer_buf.at[j, pl.ds(UNITS * i, UNITS), :], out.at[0, :, cols], out_sem.at[i, j])
            for i, out in enumerate((gate_out, up_out, down_out))
        ]

    def mean_step(i):
        j = lax.rem(i + long + 1, PIECES) if long else i
        gossip(j).wait_recv()

        def some(i):
            at = pl.ds(pl.multiple_of(i * 144, 16), 144)
            mean = (new_buf[j, at, :].astype(F32) + peer_buf[j, at, :].astype(F32)) * 0.5
            peer_buf[j, at, :] = mean.astype(BF16)

        loop(0, 3 * UNITS // 144, some)
        for copy in outs(j):
            copy.start()

    if long:
        pass_on(2)
    loop(0, PIECES, mean_step)

    for copy in (*pairs, c_across, y_sum, rows_fly):
        copy.wait_send()

    def sent(place):
        x_across(place).wait_send()
        x_sibling(place).wait_send()
        c_sibling(place).wait_send()
        part_sibling(place).wait_send()

    loop(0, 8, sent)

    def hops_sent(k):
        x_hop(True, k).wait_send()
        c_hop(True, k, 0).wait_send()
        c_hop(False, k, 1).wait_send()
        chain_hop(0, k - 1, chain.at[0, 0]).wait_send()
        chain_hop(3, k - 1, chain.at[0, 0]).wait_send()

        @pl.when(k <= 3)
        def _():
            x_hop(False, k).wait_send()
            c_hop(True, k, 1).wait_send()
            c_hop(False, k, 0).wait_send()
            chain_hop(1, k - 1, chain.at[0, 0]).wait_send()
            chain_hop(2, k - 1, chain.at[0, 0]).wait_send()

    loop(1, 5, hops_sent)

    def finish(j):
        if long:
            @pl.when(goes_long(j))
            def _():
                for hop_number in range(3):
                    long_way(hop_number, j).wait_send()

            pl.when(jnp.logical_not(goes_long(j)))(lambda: gossip(j).wait_send())
        else:
            gossip(j).wait_send()
        for copy in outs(j):
            copy.wait()

    loop(0, PIECES, finish)


def call(distance, arrays):
    dma = pltpu.SemaphoreType.DMA
    link = BF16 if distance == 2 else F32
    vmem = pl.BlockSpec(memory_space=pltpu.VMEM)
    hbm = pl.BlockSpec(memory_space=pl.ANY)
    return pl.pallas_call(
        functools.partial(kernel, distance),
        out_shape=(jax.ShapeDtypeStruct((1, 40, D), BF16),) + (jax.ShapeDtypeStruct((1, UNITS, D), BF16),) * 3,
        in_specs=[vmem, vmem, hbm, hbm, hbm],
        out_specs=(vmem, hbm, hbm, hbm),
        scratch_shapes=[
            pltpu.VMEM((TOKENS, D), BF16),
            pltpu.VMEM((TOKENS, D), BF16),
            pltpu.VMEM((3 * WIDE, D), BF16),
            pltpu.VMEM((TOKENS, 2 * WIDE), BF16),
            pltpu.VMEM((TOKENS, WIDE), BF16),
            pltpu.VMEM((3 * UNITS, TOKENS), BF16),
            pltpu.VMEM((4, PAIR, 2 * WIDE), F32),
            pltpu.VMEM((TOKENS, D), F32),
            pltpu.VMEM((TOKENS, HALF), F32),
            pltpu.VMEM((4, BLOCK, HALF), link),
            pltpu.VMEM((4, 4, BLOCK, HALF), link),
            pltpu.VMEM((PIECES, 3 * UNITS, PIECE), BF16),
            pltpu.VMEM((PIECES, 3 * UNITS, PIECE), BF16),
            pltpu.VMEM((2, LONG, 3 * UNITS, PIECE) if distance == 2 else (2, LONG, 16, 128), BF16),
            pltpu.VMEM((2, 40, D), F32),
            pltpu.VMEM((2, BLOCK, HALF), F32),
            pltpu.VMEM((BLOCK, HALF), F32),
            pltpu.VMEM((BLOCK, HALF), F32),
            pltpu.VMEM((BLOCK, HALF), F32),
            pltpu.VMEM((40, D), F32),
            dma((3,)), dma((2,)), dma((2,)),
            dma((16,)), dma((16,)), dma((16,)), dma((16,)), dma((8,)), dma((8,)), dma, dma,
            dma((8,)), dma((8,)), dma((8,)), dma((8,)), dma((8,)), dma((8,)), dma((4, 4)), dma((4, 4)),
            dma, dma, dma, dma,
            dma((PIECES,)), dma((PIECES,)), dma((3, PIECES)), dma((3, LONG)), dma((2, LONG)),
        ],
        compiler_params=pltpu.CompilerParams(
            collective_id=distance, has_side_effects=True, vmem_limit_bytes=63 * 2**20
        ),
        cost_estimate=pl.CostEstimate(flops=13600000000, bytes_accessed=10000000, transcendentals=400000),
        name=f"gossip_by_{distance}",
    )(*arrays)


def hand_over_kernel(*refs):
    sources, results, (held, in_sem, out_sem) = refs[:3], refs[3:6], refs[6:]
    spots = [(i, j, pl.ds(96 * j, 96)) for i in range(3) for j in range(3)]
    ins = [pltpu.make_async_copy(sources[i].at[0, at, :], held.at[i, at, :], in_sem.at[i, j]) for i, j, at in spots]
    outs = [pltpu.make_async_copy(held.at[i, at, :], results[i].at[0, at, :], out_sem.at[i, j]) for i, j, at in spots]
    for copy in ins:
        copy.start()
    for arrived, leaving in zip(ins, outs):
        arrived.wait()
        leaving.start()
    for copy in outs:
        copy.wait()


def hand_over(arrays):
    hbm = pl.BlockSpec(memory_space=pl.ANY)
    return pl.pallas_call(
        hand_over_kernel,
        out_shape=(jax.ShapeDtypeStruct((1, UNITS, D), BF16),) * 3,
        in_specs=[hbm] * 3,
        out_specs=(hbm,) * 3,
        scratch_shapes=[
            pltpu.VMEM((3, UNITS, D), BF16),
            pltpu.SemaphoreType.DMA((3, 3)),
            pltpu.SemaphoreType.DMA((3, 3)),
        ],
        compiler_params=pltpu.CompilerParams(vmem_limit_bytes=63 * 2**20),
        name="hand_over",
    )(*arrays)


def body(inputs, cotangent, gate_weight, up_weight, down_weight, step):
    arrays = (
        inputs, cotangent, jnp.swapaxes(gate_weight, 1, 2), jnp.swapaxes(up_weight, 1, 2), down_weight,
    )
    branches = [functools.partial(call, 1 << power) for power in range(3)]
    grad, *means = lax.switch(step[0] % 3, branches, arrays)
    gate, up, down = hand_over(means)
    return grad, jnp.swapaxes(gate, 1, 2), jnp.swapaxes(up, 1, 2), down


def solution(mesh):
    in_specs = (
        P("replica", "tensor", None),
        P("replica", "tensor", None),
        P("replica", None, "tensor"),
        P("replica", None, "tensor"),
        P("replica", "tensor", None),
        P(),
    )
    out_specs = (
        P("replica", "tensor", None),
        P("replica", None, "tensor"),
        P("replica", None, "tensor"),
        P("replica", "tensor", None),
    )
    return jax.shard_map(body, mesh=mesh, in_specs=in_specs, out_specs=out_specs, check_vma=False)
```

time: 461 us -> 175 us (0.38)
  waiting for transfers between devices: 380 us -> 0 us
  Pallas kernels: 0 us -> 173 us
  matrix products: 38.8 us -> 0 us
  starting transfers between devices: 14 us -> 0 us
  between operations: 14.6 us -> 1.31 us
  other arithmetic: 6.99 us -> 0 us
  local copies, waits for them, and re-layouts: 5.96 us -> 0.68 us
    all_gather x2 -> x0, waiting for transfers between devices: 182 us -> none  [the longest x1 99.2 us: body(): whole = lax.all_gather(rows, 'tensor', axis=0, tiled=True)]
    pallas_call x0 -> x2, Pallas kernels: none -> 173 us  [the longest x1 169 us: call(): pl.pallas_call(functools.partial(kernel, distance), out_shape=(jax.ShapeD...]
    ppermute x2 -> x0, waiting for transfers between devices: 106 us -> none  [shifted(): lax.ppermute(array, axis, [(i, (i + by) % peers) for i in range(peers)])]
    reduce_scatter x1 -> x0, waiting for transfers between devices: 80.7 us -> none  [body(): lax.psum_scatter(term, 'tensor', scatter_dimension=1, tiled=True)]
    dot_general x8 -> x0, matrix products: 38.8 us -> none  [the longest x3 16.4 us: contract_cols(): lax.dot_general(left, right, (((1,), (1,)), ((), ())), preferred_element_...]
    all_to_all x1 -> x0, starting transfers between devices: 10.3 us -> none  [body(): lax.all_to_all(columns, 'tensor', split_axis=0, concat_axis=1, tiled=True)]
    all_to_all x1 -> x0, waiting for transfers between devices: 10.1 us -> none  [body(): lax.all_to_all(columns, 'tensor', split_axis=0, concat_axis=1, tiled=True)]
  transfers between devices with their start and end apart: 6 -> 0, of which waited for: 5 -> 0; matrix products, arithmetic and copies ran while one was open for 7% -> 0% of each run, Pallas kernels for 0% -> 0%
where the time goes in v1:
time: 175 us
  Pallas kernels  173 us (99%)
    pallas_call x1, Pallas kernels, call(): pl.pallas_call(functools.partial(kernel, distance), out_shape=(jax.ShapeD...  169 us

profile of v1, /device:TPU:1, one launch (start us, length us, event | category | flops | bytes accessed | tf_op | source)
XLA Modules:
  0.0 174.8 jit_solution(17125628415937580196)
XLA Ops:
  1.3 169.4 %conditional.1 = ((bf16[1,40,2304]{2,1,0:T(8,128)(2,1)S(1)}, bf16[1,288,2304]{2,1,0:T(8,128)(2,1)}, bf16[1,288,2304]{2,1,0:T(8,128)(2,1)}, bf16[1,288,2304]{2,1,0:T(8,128)(2,1)})) conditional(s32[]{:T(128)} %clamp.3, (bf16[1,40,2304]{2,1,0:T(8,128)(2,1)}, bf16[1,40,2304]{2,1,0:T(8,128)(2,1)}, bf16[1,288,2304]{2,1,0:T(8,128)(2,1)}, ...), branch_computations={%region_0.1_spmd, %region_1.2_spmd, %region_2.3_spmd} | conditional | flops 13600000000 | bytes 10000008 | solution.py:544
  1.3 169.2 %gossip_by_1.1 = (bf16[1,40,2304]{2,1,0:T(8,128)(2,1)S(1)}, bf16[1,288,2304]{2,1,0:T(8,128)(2,1)}, bf16[1,288,2304]{2,1,0:T(8,128)(2,1)}, bf16[1,288,2304]{2,1,0:T(8,128)(2,1)}) custom-call(bf16[1,40,2304]{2,1,0:T(8,128)(2,1)} %get-tuple-element.30.x_in, bf16[1,40,2304]{2,1,0:T(8,128)(2,1)} %get-tuple-element.31.cot_in, ...), custom_call_target="tpu_custom_call" | custom-call | flops 13600000000 | bytes 10000000 | tf_op jit(solution)/shard_map/cond/branch_0_fun/gossip_by_1/pallas_call | solution.py:468
  170.7 3.4 %hand_over.1 = (bf16[1,288,2304]{2,1,0:T(8,128)(2,1)}, bf16[1,288,2304]{2,1,0:T(8,128)(2,1)}, bf16[1,288,2304]{2,1,0:T(8,128)(2,1)}) custom-call(bf16[1,288,2304]{2,1,0:T(8,128)(2,1)} %get-tuple-element.57.refs_0_, bf16[1,288,2304]{2,1,0:T(8,128)(2,1)} %get-tuple-element.58.refs_1_, bf16[1,288,2304]{2,1,0:T(8,128)(2,1)} %get-tuple-element.59.refs_2_), custom_call_target="tpu_custom_call" | custom-call | tf_op jit(solution)/shard_map/hand_over/pallas_call | solution.py:524
  174.1 0.7 copy.24

commit v2 on v1

--- a/solution.py
+++ b/solution.py
@@ -92,6 +92,7 @@
     takes_from = (lax.rem(r + distance, 8), t)
 
     long = LONG if distance == 2 else 0
+    early = EARLY + (1 if long else 0)
     onward = (r, lax.rem(z + 1 + 6 * c, 8) * 4 + base)
     backward_on = (r, lax.rem(z + 7 - 6 * c, 8) * 4 + base)
 
@@ -178,6 +179,8 @@
 
     for i in range(3):
         weights[pl.ds(WIDE * i + UNITS, WIDE - UNITS), :] = jnp.zeros((WIDE - UNITS, D), BF16)
+    for forward in (True, False):
+        c_hop(forward, 1, 0).start()
     for load in loads:
         load.wait()
 
@@ -274,84 +277,12 @@
         loop(0, BLOCK // 16, some)
 
     def start_chains():
-        for p in (5, 6, 7):
+        for p in range(8):
             part_sibling(p).wait_recv()
         for n, (_, pair, _) in enumerate(chains):
             place = stop_place(n, 0)
             add_share(lead.at[n], None, place, pair)
             chain_hop(n, 0, lead.at[n]).start()
-
-    def places(k, work):
-        loop(jnp.maximum(2 * k - 1, 0), jnp.where(k < 0, 0, jnp.minimum(2 * k + 1, 8)), work)
-
-    def step(k):
-        @pl.when(k <= 4)
-        def _():
-            x_hop(True, k).wait_recv()
-
-            @pl.when(k <= 3)
-            def _():
-                x_hop(True, k + 1).start()
-
-            x_across(first_place(k)).start()
-
-            @pl.when(k <= 3)
-            def _():
-                x_hop(False, k).wait_recv()
-
-                @pl.when(k <= 2)
-                def _():
-                    x_hop(False, k + 1).start()
-
-                x_across(second_place(k)).start()
-
-        def from_across(place):
-            x_across(place).wait_recv()
-            x_sibling(place).start()
-
-        def take_c(forward, pair):
-            far = forward == (pair == 0)
-
-            @pl.when(k <= (5 if far else 4))
-            def _():
-                @pl.when(k >= 2)
-                def _():
-                    c_hop(forward, k - 1, pair).wait_recv()
-
-                @pl.when(k <= (4 if far else 3))
-                def _():
-                    c_hop(forward, k, pair).start()
-
-        places(k - 1, from_across)
-        take_c(True, 0)
-        take_c(False, 0)
-        places(k - 1, forward_a)
-        places(k - 2, forward_b)
-
-        @pl.when(k == 1)
-        def _():
-            c_across.wait_recv()
-
-        take_c(False, 1)
-        take_c(True, 1)
-        places(k - 1, lambda place: c_sibling(place).start())
-        places(k - 2, turn_pair)
-
-        @pl.when(k == 7)
-        def _():
-            backward(7)
-            start_chains()
-
-        loop(jnp.where(k == 7, EARLY, 0), jnp.where(k == 7, PIECES, jnp.where(k == 6, EARLY, 0)), update)
-
-        @pl.when(k < 7)
-        def _():
-            places(k - 3, backward)
-
-    loop(1, 8, step)
-
-    for p in range(5):
-        part_sibling(p).wait_recv()
 
     def chain_step(m):
         for n, (_, pair, stops) in enumerate(chains):
@@ -363,58 +294,104 @@
 
             if stops == 4:
                 go()
-            elif isinstance(m, int):
-                if m < stops:
-                    go()
             else:
                 pl.when(m < stops)(go)
 
-    if long:
-        loop(1, 3, chain_step)
-        pass_on(1)
-        chain_step(3)
-    else:
-        loop(1, 4, chain_step)
+    def places(k, work):
+        loop(jnp.maximum(2 * k - 1, 0), jnp.where(k < 0, 0, jnp.minimum(2 * k + 1, 8)), work)
+
+    def step(k):
+        @pl.when(k <= 4)
+        def _():
+            x_hop(True, k).wait_recv()
+
+            @pl.when(k <= 3)
+            def _():
+                x_hop(True, k + 1).start()
+
+            x_across(first_place(k)).start()
+
+            @pl.when(k <= 3)
+            def _():
+                x_hop(False, k).wait_recv()
+
+                @pl.when(k <= 2)
+                def _():
+                    x_hop(False, k + 1).start()
+
+                x_across(second_place(k)).start()
+
+        def from_across(place):
+            x_across(place).wait_recv()
+            x_sibling(place).start()
+
+        def take_c(forward, pair):
+            far = forward == (pair == 0)
+
+            @pl.when(k <= (5 if far else 4))
+            def _():
+                @pl.when(k >= 2)
+                def _():
+                    c_hop(forward, k - 1, pair).wait_recv()
+
+                @pl.when(jnp.logical_and(k <= (4 if far else 3), k >= (2 if pair == 0 else 1)))
+                def _():
+                    c_hop(forward, k, pair).start()
+
+        places(k - 1, from_across)
+        take_c(True, 0)
+        take_c(False, 0)
+        places(k - 1, forward_a)
+
+        @pl.when(k == 1)
+        def _():
+            c_across.wait_recv()
+
+        take_c(False, 1)
+        take_c(True, 1)
+        places(k - 1, lambda place: c_sibling(place).start())
+        places(k - 2, forward_b)
+        places(k - 2, turn_pair)
+
+        @pl.when(k == 7)
+        def _():
+            backward(7)
+            start_chains()
+
+        @pl.when(k >= 8)
+        def _():
+            chain_step(k - 7)
+            if long:
+                pl.when(k == 8)(lambda: pass_on(1))
+
+        done = jnp.where(k >= 8, early + 2 * (k - 8), 0)
+        goal = jnp.where(k >= 8, jnp.minimum(done + 2, PIECES), jnp.where(k == 6, early, 0))
+        loop(done, goal, update)
+
+        @pl.when(k < 7)
+        def _():
+            places(k - 3, backward)
+
+    loop(1, 11, step)
+
     for n in (1, 3):
         chain_hop(n, chains[n][2] - 1, chain.at[n, 0]).wait_recv()
     add_share(ysend, lambda i: chain[1, 2, i, :].astype(F32) + chain[3, 3, i, :].astype(F32), 0, 1)
     y_sum = remote(ysend, ybuf, ys_ss, ys_rs, across)
     y_sum.start()
+    if long:
+        pass_on(2)
     for n in (0, 2):
         chain_hop(n, chains[n][2] - 1, chain.at[n, 0]).wait_recv()
     add_share(fin, lambda i: chain[0, 3, i, :].astype(F32) + chain[2, 2, i, :].astype(F32), 0, 0)
     y_sum.wait_recv()
-    fin[...] = (fin[...] + ybuf[...]) * scale_model
+    fin[...] = (fin[...] + ybuf[...].astype(F32)) * scale_model
     theirs = pl.ds(pl.multiple_of((1 - c) * 40, 8), 40)
     rows_fly = remote(fin.at[theirs, :], rows32.at[:, mine], f_ss, f_rs, sibling)
     rows_fly.start()
     rows32[:, mine] = fin[forty, :]
     rows_fly.wait_recv()
     grad_out[0] = rows32[...].astype(BF16)
-
-    def outs(j):
-        cols = pl.ds(pl.multiple_of(j * PIECE, PIECE), PIECE)
-        return [
-            pltpu.make_async_copy(peer_buf.at[j, pl.ds(UNITS * i, UNITS), :], out.at[0, :, cols], out_sem.at[i, j])
-            for i, out in enumerate((gate_out, up_out, down_out))
-        ]
-
-    def mean_step(i):
-        j = lax.rem(i + long + 1, PIECES) if long else i
-        gossip(j).wait_recv()
-
-        def some(i):
-            at = pl.ds(pl.multiple_of(i * 144, 16), 144)
-            mean = (new_buf[j, at, :].astype(F32) + peer_buf[j, at, :].astype(F32)) * 0.5
-            peer_buf[j, at, :] = mean.astype(BF16)
-
-        loop(0, 3 * UNITS // 144, some)
-        for copy in outs(j):
-            copy.start()
-
-    if long:
-        pass_on(2)
-    loop(0, PIECES, mean_step)
 
     for copy in (*pairs, c_across, y_sum, rows_fly):
         copy.wait_send()
@@ -444,6 +421,28 @@
 
     loop(1, 5, hops_sent)
 
+    def outs(j):
+        cols = pl.ds(pl.multiple_of(j * PIECE, PIECE), PIECE)
+        return [
+            pltpu.make_async_copy(peer_buf.at[j, pl.ds(UNITS * i, UNITS), :], out.at[0, :, cols], out_sem.at[i])
+            for i, out in enumerate((gate_out, up_out, down_out))
+        ]
+
+    def mean_step(i):
+        j = lax.rem(i + long + 1, PIECES) if long else i
+        gossip(j).wait_recv()
+
+        def some(i):
+            at = pl.ds(pl.multiple_of(i * 144, 16), 144)
+            mean = (new_buf[j, at, :].astype(F32) + peer_buf[j, at, :].astype(F32)) * 0.5
+            peer_buf[j, at, :] = mean.astype(BF16)
+
+        loop(0, 3 * UNITS // 144, some)
+        for copy in outs(j):
+            copy.start()
+
+    loop(0, PIECES, mean_step)
+
     def finish(j):
         if long:
             @pl.when(goes_long(j))
@@ -454,15 +453,16 @@
             pl.when(jnp.logical_not(goes_long(j)))(lambda: gossip(j).wait_send())
         else:
             gossip(j).wait_send()
-        for copy in outs(j):
-            copy.wait()
 
     loop(0, PIECES, finish)
+    for i, out in enumerate((gate_out, up_out, down_out)):
+        pltpu.make_async_copy(out.at[0], out.at[0], out_sem.at[i]).wait()
 
 
 def call(distance, arrays):
     dma = pltpu.SemaphoreType.DMA
     link = BF16 if distance == 2 else F32
+    y_link = BF16 if distance == 1 else F32
     vmem = pl.BlockSpec(memory_space=pltpu.VMEM)
     hbm = pl.BlockSpec(memory_space=pl.ANY)
     return pl.pallas_call(
@@ -487,15 +487,15 @@
             pltpu.VMEM((2, LONG, 3 * UNITS, PIECE) if distance == 2 else (2, LONG, 16, 128), BF16),
             pltpu.VMEM((2, 40, D), F32),
             pltpu.VMEM((2, BLOCK, HALF), F32),
-            pltpu.VMEM((BLOCK, HALF), F32),
-            pltpu.VMEM((BLOCK, HALF), F32),
+            pltpu.VMEM((BLOCK, HALF), y_link),
+            pltpu.VMEM((BLOCK, HALF), y_link),
             pltpu.VMEM((BLOCK, HALF), F32),
             pltpu.VMEM((40, D), F32),
             dma((3,)), dma((2,)), dma((2,)),
             dma((16,)), dma((16,)), dma((16,)), dma((16,)), dma((8,)), dma((8,)), dma, dma,
             dma((8,)), dma((8,)), dma((8,)), dma((8,)), dma((8,)), dma((8,)), dma((4, 4)), dma((4, 4)),
             dma, dma, dma, dma,
-            dma((PIECES,)), dma((PIECES,)), dma((3, PIECES)), dma((3, LONG)), dma((2, LONG)),
+            dma((PIECES,)), dma((PIECES,)), dma((3,)), dma((3, LONG)), dma((2, LONG)),
         ],
         compiler_params=pltpu.CompilerParams(
             collective_id=distance, has_side_effects=True, vmem_limit_bytes=63 * 2**20

time: 175 us -> 162 us (0.926)
  Pallas kernels: 173 us -> 159 us
    pallas_call x1, Pallas kernels: 169 us -> 156 us  [call(): pl.pallas_call(functools.partial(kernel, distance), out_shape=(jax.ShapeD...]
where the time goes in v2:
time: 162 us
  Pallas kernels  159 us (98%)
    pallas_call x1, Pallas kernels, call(): pl.pallas_call(functools.partial(kernel, distance), out_shape=(jax.ShapeD...  156 us
    pallas_call x1, Pallas kernels, hand_over(): pl.pallas_call(hand_over_kernel, out_shape=(jax.ShapeDtypeStruct((1, UNIT...  3.4 us

profile of v2, /device:TPU:1, one launch (start us, length us, event | category | flops | bytes accessed | tf_op | source)
XLA Modules:
  0.0 161.8 jit_solution(5588637854433005989)
XLA Ops:
  1.3 156.4 %conditional.1 = ((bf16[1,40,2304]{2,1,0:T(8,128)(2,1)S(1)}, bf16[1,288,2304]{2,1,0:T(8,128)(2,1)}, bf16[1,288,2304]{2,1,0:T(8,128)(2,1)}, bf16[1,288,2304]{2,1,0:T(8,128)(2,1)})) conditional(s32[]{:T(128)} %clamp.3, (bf16[1,40,2304]{2,1,0:T(8,128)(2,1)}, bf16[1,40,2304]{2,1,0:T(8,128)(2,1)}, bf16[1,288,2304]{2,1,0:T(8,128)(2,1)}, ...), branch_computations={%region_0.1_spmd, %region_1.2_spmd, %region_2.3_spmd} | conditional | flops 13600000000 | bytes 10000008 | solution.py:544
  1.5 155.9 %gossip_by_4.1 = (bf16[1,40,2304]{2,1,0:T(8,128)(2,1)S(1)}, bf16[1,288,2304]{2,1,0:T(8,128)(2,1)}, bf16[1,288,2304]{2,1,0:T(8,128)(2,1)}, bf16[1,288,2304]{2,1,0:T(8,128)(2,1)}) custom-call(bf16[1,40,2304]{2,1,0:T(8,128)(2,1)} %get-tuple-element.40.x_in, bf16[1,40,2304]{2,1,0:T(8,128)(2,1)} %get-tuple-element.41.cot_in, ...), custom_call_target="tpu_custom_call" | custom-call | flops 13600000000 | bytes 10000000 | tf_op jit(solution)/shard_map/cond/branch_2_fun/gossip_by_4/pallas_call | solution.py:468
  157.7 3.4 %hand_over.1 = (bf16[1,288,2304]{2,1,0:T(8,128)(2,1)}, bf16[1,288,2304]{2,1,0:T(8,128)(2,1)}, bf16[1,288,2304]{2,1,0:T(8,128)(2,1)}) custom-call(bf16[1,288,2304]{2,1,0:T(8,128)(2,1)} %get-tuple-element.57.refs_0_, bf16[1,288,2304]{2,1,0:T(8,128)(2,1)} %get-tuple-element.58.refs_1_, bf16[1,288,2304]{2,1,0:T(8,128)(2,1)} %get-tuple-element.59.refs_2_), custom_call_target="tpu_custom_call" | custom-call | tf_op jit(solution)/shard_map/hand_over/pallas_call | solution.py:524
  161.1 0.7 copy.24

commit v3 on v2

--- a/solution.py
+++ b/solution.py
@@ -338,7 +338,14 @@
                 def _():
                     c_hop(forward, k, pair).start()
 
+        places(k - 2, forward_b)
         places(k - 1, from_across)
+        places(k - 2, turn_pair)
+
+        @pl.when(k < 6)
+        def _():
+            places(k - 3, backward)
+
         take_c(True, 0)
         take_c(False, 0)
         places(k - 1, forward_a)
@@ -350,12 +357,10 @@
         take_c(False, 1)
         take_c(True, 1)
         places(k - 1, lambda place: c_sibling(place).start())
-        places(k - 2, forward_b)
-        places(k - 2, turn_pair)
 
         @pl.when(k == 7)
         def _():
-            backward(7)
+            loop(5, 8, backward)
             start_chains()
 
         @pl.when(k >= 8)
@@ -367,10 +372,6 @@
         done = jnp.where(k >= 8, early + 2 * (k - 8), 0)
         goal = jnp.where(k >= 8, jnp.minimum(done + 2, PIECES), jnp.where(k == 6, early, 0))
         loop(done, goal, update)
-
-        @pl.when(k < 7)
-        def _():
-            places(k - 3, backward)
 
     loop(1, 11, step)
 

time: 162 us -> 165 us (1.019)
  Pallas kernels: 159 us -> 162 us
    pallas_call x1, Pallas kernels: 156 us -> 158 us  [call(): pl.pallas_call(functools.partial(kernel, distance), out_shape=(jax.ShapeD...]
where the time goes in v3:
time: 165 us; the launch traced here: 164 us
  Pallas kernels  162 us (98%)
    pallas_call x1, Pallas kernels, call(): pl.pallas_call(functools.partial(kernel, distance), out_shape=(jax.ShapeD...  158 us
    pallas_call x1, Pallas kernels, hand_over(): pl.pallas_call(hand_over_kernel, out_shape=(jax.ShapeDtypeStruct((1, UNIT...  3.4 us

profile of v3, /device:TPU:1, one launch (start us, length us, event | category | flops | bytes accessed | tf_op | source)
XLA Modules:
  0.0 164.0 jit_solution(2905180294259191018)
XLA Ops:
  1.3 158.6 %conditional.1 = ((bf16[1,40,2304]{2,1,0:T(8,128)(2,1)S(1)}, bf16[1,288,2304]{2,1,0:T(8,128)(2,1)}, bf16[1,288,2304]{2,1,0:T(8,128)(2,1)}, bf16[1,288,2304]{2,1,0:T(8,128)(2,1)})) conditional(s32[]{:T(128)} %clamp.3, (bf16[1,40,2304]{2,1,0:T(8,128)(2,1)}, bf16[1,40,2304]{2,1,0:T(8,128)(2,1)}, bf16[1,288,2304]{2,1,0:T(8,128)(2,1)}, ...), branch_computations={%region_0.1_spmd, %region_1.2_spmd, %region_2.3_spmd} | conditional | flops 13600000000 | bytes 10000008 | solution.py:545
  1.3 158.4 %gossip_by_1.1 = (bf16[1,40,2304]{2,1,0:T(8,128)(2,1)S(1)}, bf16[1,288,2304]{2,1,0:T(8,128)(2,1)}, bf16[1,288,2304]{2,1,0:T(8,128)(2,1)}, bf16[1,288,2304]{2,1,0:T(8,128)(2,1)}) custom-call(bf16[1,40,2304]{2,1,0:T(8,128)(2,1)} %get-tuple-element.30.x_in, bf16[1,40,2304]{2,1,0:T(8,128)(2,1)} %get-tuple-element.31.cot_in, ...), custom_call_target="tpu_custom_call" | custom-call | flops 13600000000 | bytes 10000000 | tf_op jit(solution)/shard_map/cond/branch_0_fun/gossip_by_1/pallas_call | solution.py:469
  159.9 3.4 %hand_over.1 = (bf16[1,288,2304]{2,1,0:T(8,128)(2,1)}, bf16[1,288,2304]{2,1,0:T(8,128)(2,1)}, bf16[1,288,2304]{2,1,0:T(8,128)(2,1)}) custom-call(bf16[1,288,2304]{2,1,0:T(8,128)(2,1)} %get-tuple-element.57.refs_0_, bf16[1,288,2304]{2,1,0:T(8,128)(2,1)} %get-tuple-element.58.refs_1_, bf16[1,288,2304]{2,1,0:T(8,128)(2,1)} %get-tuple-element.59.refs_2_), custom_call_target="tpu_custom_call" | custom-call | tf_op jit(solution)/shard_map/hand_over/pallas_call | solution.py:525
  163.3 0.7 copy.24
